TPU v7x, 128 devices: a whole 4x4x4 slice. The times are simulated.
128 devices in a mesh: grp: 4 (over y), ep: 32 (over z, x, core).
Axes of the slice: x: 4, y: 4, z: 4, core: 2. Of those that a mesh axis runs over, the one named last changes fastest.
Arguments:
- hidden: bfloat16 [1024, 2, 3584], P(('grp', 'ep')), may hold values from -6 to 6
- norm_gain: float32 [3584], replicated, may hold values from 0.5 to 1.5
- route_ids: int32 [1024, 2, 8], P(('grp', 'ep')), may hold values from 0 to 127, all different within a row; in each aligned block of 16 rows (0 to 15, 16 to 31, ..., all dimensions but the last counted through in order) at most 2 rows name the same one
- gate_weights: float32 [1024, 2, 8], P(('grp', 'ep')), may hold values from 0.1 to 0.5
- w_gate: bfloat16 [128, 3584, 1024], P(('grp', 'ep')), may hold values from -0.09375 to 0.09375
- w_up: bfloat16 [128, 3584, 1024], P(('grp', 'ep')), may hold values from -0.09375 to 0.09375
- w_down: bfloat16 [128, 1024, 3584], P(('grp', 'ep')), may hold values from -0.1875 to 0.1875
Outputs:
- moe_out: bfloat16 [1024, 2, 3584], P(('grp', 'ep'))
Inputs may be any that keep to these rules, and one draw needn't show every extreme that they name: `route_ids`: each row names 8 distinct experts; among the 16 rows of one device (all steps together) no expert is named more than 2 times, a bound that some block reaches.
All inputs are finite; a program needn't handle non-finite values.
Results may differ from a plain program's by a relative error of at most 0.0071.
Values may be sent and summed in bfloat16 or wider, within the bound.
A program may use at most 128 MiB of HBM per device.

v0:
```python
import jax
import jax.numpy as jnp
from jax import lax
from jax.sharding import PartitionSpec as P


def slot_plan(route_rows, gate_rows, experts, most):
    count, topk = route_rows.shape
    flat_routes = route_rows.reshape(-1)
    flat_gates = gate_rows.reshape(-1)
    assigned = flat_routes.shape[0]
    onehot = (flat_routes[:, None] == lax.broadcasted_iota(jnp.int32, (1, experts), 1)).astype(
        jnp.int32
    )
    earlier = jnp.cumsum(onehot, axis=0) - onehot
    rank = jnp.sum(earlier * onehot, axis=1)
    slot = flat_routes * most + rank
    placing = (slot[:, None] == lax.broadcasted_iota(jnp.int32, (1, experts * most), 1)).astype(
        jnp.float32
    )
    owner = lax.broadcasted_iota(jnp.int32, (assigned, 1), 0) // topk
    row_pick = (owner == lax.broadcasted_iota(jnp.int32, (1, count), 1)).astype(jnp.float32)
    send_matrix = jnp.dot(
        placing.T.astype(jnp.bfloat16),
        row_pick.astype(jnp.bfloat16),
        preferred_element_type=jnp.float32,
    ).astype(jnp.bfloat16)
    combine_matrix = jnp.dot(
        row_pick.T, placing * flat_gates[:, None], precision=lax.Precision.HIGHEST
    )
    return (send_matrix, combine_matrix)


def run_experts(arrived, w_gate, w_up, w_down):
    gate_part = jnp.einsum("pxmd,xdf->pxmf", arrived, w_gate, preferred_element_type=jnp.float32)
    up_part = jnp.einsum("pxmd,xdf->pxmf", arrived, w_up, preferred_element_type=jnp.float32)
    act = (jax.nn.silu(gate_part) * up_part).astype(jnp.bfloat16)
    return jnp.einsum("pxmf,xfd->pxmd", act, w_down, preferred_element_type=jnp.float32).astype(
        jnp.bfloat16
    )


def mixture(normed_rows, route_rows, gate_rows, w_gate, w_up, w_down, most):
    groups = lax.axis_size("grp")
    members = lax.axis_size("ep")
    local = w_gate.shape[0]
    experts = local * groups * members
    dmodel = normed_rows.shape[1]
    send_matrix, combine_matrix = slot_plan(route_rows, gate_rows, experts, most)
    outgoing = jnp.dot(send_matrix, normed_rows, preferred_element_type=jnp.float32).astype(
        jnp.bfloat16
    )
    shaped = outgoing.reshape(groups * members, local, most, dmodel)
    came_back = lax.all_to_all(
        run_experts(
            lax.all_to_all(shaped, ("grp", "ep"), split_axis=0, concat_axis=0, tiled=True),
            w_gate,
            w_up,
            w_down,
        ),
        ("grp", "ep"),
        split_axis=0,
        concat_axis=0,
        tiled=True,
    )
    flat_back = came_back.reshape(experts * most, dmodel).astype(jnp.float32)
    return jnp.dot(combine_matrix, flat_back, precision=lax.Precision.HIGHEST)


def body(hidden, norm_gain, route_ids, gate_weights, w_gate, w_up, w_down):
    rows, steps, dmodel = hidden.shape
    topk = route_ids.shape[2]
    experts = w_gate.shape[0] * lax.axis_size("grp") * lax.axis_size("ep")
    most = max(2, rows * steps * topk // experts)
    widened = hidden.astype(jnp.float32)
    scale_rows = lax.rsqrt(jnp.mean(widened * widened, axis=-1, keepdims=True) + 1e-06)
    normed = (widened * scale_rows * norm_gain).astype(jnp.bfloat16)
    results = [
        mixture(
            normed[:, step_index],
            route_ids[:, step_index],
            gate_weights[:, step_index],
            w_gate,
            w_up,
            w_down,
            most,
        )
        for step_index in range(steps)
    ]
    mixed = jnp.stack(results, axis=1)
    return mixed.astype(jnp.bfloat16)


def solution(mesh):
    placed = (
        P(("grp", "ep"), None, None),
        P(),
        P(("grp", "ep"), None, None),
        P(("grp", "ep"), None, None),
        P(("grp", "ep"), None, None),
        P(("grp", "ep"), None, None),
        P(("grp", "ep"), None, None),
    )
    return jax.shard_map(
        body, mesh=mesh, in_specs=placed, out_specs=P(("grp", "ep"), None, None), check_vma=False
    )
```

profile of v0, /device:TPU:1, one launch (start us, length us, event | category | flops | bytes accessed | tf_op | source)
XLA Modules:
  0.0 150.0 jit_solution(2006772914032999126)
XLA Ops:
  1.7 1.0 fusion.84
  2.7 1.0 fusion.86
  4.7 1.7 %reshape.112 = bf16[128,1,2,3584]{3,2,0,1:T(2,128)(2,1)} reshape(bf16[256,3584]{1,0:T(8,128)(2,1)S(1)} %convolution_convert_fusion.1) | data formatting | bytes 3670016 | tf_op jit(solution)/shard_map/reshape | solution.py:53
  6.4 11.9 %all-to-all-start = ((bf16[128,1,2,3584]{3,2,1,0:T(2,128)(2,1)}), bf16[128,1,2,3584]{3,2,1,0:T(2,128)(2,1)}, u32[]{:S(2)}, u32[]{:S(2)}) async-start(bf16[128,1,2,3584]{3,2,1,0:T(2,128)(2,1)} %bitcast.1), calls=%async_computation | async-start | bytes 3670016 | tf_op jit(solution)/shard_map/all_to_all | solution.py:56
  19.2 1.7 %reshape.119 = bf16[128,1,2,3584]{3,2,0,1:T(2,128)(2,1)} reshape(bf16[256,3584]{1,0:T(8,128)(2,1)S(1)} %convolution_convert_fusion) | data formatting | bytes 3670016 | tf_op jit(solution)/shard_map/reshape | solution.py:53
  20.9 24.8 %all-to-all-done = bf16[128,1,2,3584]{3,2,1,0:T(2,128)(2,1)} async-done(((bf16[128,1,2,3584]{3,2,1,0:T(2,128)(2,1)}), bf16[128,1,2,3584]{3,2,1,0:T(2,128)(2,1)}, u32[]{:S(2)}, u32[]{:S(2)}) %all-to-all-start) | async-done | bytes 1835040 | tf_op jit(solution)/shard_map/all_to_all | solution.py:56
  45.7 4.3 %all-to-all-start.2 = ((bf16[128,1,2,3584]{3,2,1,0:T(2,128)(2,1)}), bf16[128,1,2,3584]{3,2,1,0:T(2,128)(2,1)S(1)}, u32[]{:S(2)}, u32[]{:S(2)}) async-start(bf16[128,1,2,3584]{3,2,1,0:T(2,128)(2,1)} %bitcast.23), calls=%async_computation.2 | async-start | bytes 3670016 | tf_op jit(solution)/shard_map/all_to_all | solution.py:56
  50.1 5.8 %fusion.34 = f32[128,1,2,1024]{3,0,2,1:T(8,128)S(1)} fusion(bf16[1,3584,1024]{2,1,0:T(8,128)(2,1)} %param.11, bf16[128,1,2,3584]{3,2,1,0:T(2,128)(2,1)} %all-to-all-done), kind=kOutput, calls=%fused_computation.30 | convolution fusion | flops 1879048192 | bytes 10223616 | tf_op jit(solution)/shard_map/pxmd,xdf->pxmf/dot_general | solution.py:35
  55.9 6.0 %fusion.74 = bf16[128,2,1024]{2,0,1:T(8,128)(2,1)S(1)} fusion(bf16[1,3584,1024]{2,1,0:T(8,128)(2,1)} %param.12, bf16[128,1,2,3584]{3,2,1,0:T(2,128)(2,1)} %all-to-all-done, f32[128,1,2,1024]{3,0,2,1:T(8,128)S(1)} %fusion.34), kind=kOutput, calls=%fused_computation.38 | convolution fusion | flops 1880621056 | bytes 10747904 | tf_op jit(solution)/shard_map/pxmd,xdf->pxmf/dot_general | solution.py:36
  61.9 2.1 %fusion.21 = bf16[128,1,2,3584]{3,0,2,1:T(8,128)(2,1)S(1)} fusion(bf16[128,2,1024]{2,0,1:T(8,128)(2,1)S(1)} %fusion.74, bf16[1,1024,3584]{2,1,0:T(8,128)(2,1)S(1)} %bitcast.147), kind=kOutput, calls=%fused_computation.17 | convolution fusion | flops 1879965696 | bytes 9699328 | tf_op jit(solution)/shard_map/pxmf,xfd->pxmd/dot_general | solution.py:38
  64.0 3.1 %copy.20 = bf16[128,1,2,3584]{3,2,1,0:T(2,128)(2,1)} copy(bf16[128,1,2,3584]{3,0,2,1:T(8,128)(2,1)S(1)} %fusion.21) | data formatting | bytes 3670016 | tf_op jit(solution)/shard_map/convert_element_type | solution.py:38
  67.1 10.8 %all-to-all-done.2 = bf16[128,1,2,3584]{3,2,1,0:T(2,128)(2,1)S(1)} async-done(((bf16[128,1,2,3584]{3,2,1,0:T(2,128)(2,1)}), bf16[128,1,2,3584]{3,2,1,0:T(2,128)(2,1)S(1)}, u32[]{:S(2)}, u32[]{:S(2)}) %all-to-all-start.2) | async-done | bytes 1835040 | tf_op jit(solution)/shard_map/all_to_all | solution.py:56
  78.0 1.3 copy-done
  79.2 4.3 %all-to-all-start.1 = ((bf16[128,1,2,3584]{3,2,1,0:T(2,128)(2,1)}), bf16[128,1,2,3584]{3,2,1,0:T(2,128)(2,1)S(1)}, u32[]{:S(2)}, u32[]{:S(2)}) async-start(bf16[128,1,2,3584]{3,2,1,0:T(2,128)(2,1)} %copy.20), calls=%async_computation.1 | async-start | bytes 3670016 | tf_op jit(solution)/shard_map/all_to_all | solution.py:54
  83.6 5.8 %fusion.39 = f32[128,1,2,1024]{3,0,2,1:T(8,128)S(1)} fusion(bf16[1,3584,1024]{2,1,0:T(8,128)(2,1)} %param.11, bf16[128,1,2,3584]{3,2,1,0:T(2,128)(2,1)} %copy-done), kind=kOutput, calls=%fused_computation.31 | convolution fusion | flops 1879048192 | bytes 10223616 | tf_op jit(solution)/shard_map/pxmd,xdf->pxmf/dot_general | solution.py:35
  89.4 5.4 %fusion.79 = bf16[128,2,1024]{2,0,1:T(8,128)(2,1)S(1)} fusion(bf16[1,3584,1024]{2,1,0:T(8,128)(2,1)} %param.12, bf16[128,1,2,3584]{3,2,1,0:T(2,128)(2,1)S(1)} %copy-done.1, f32[128,1,2,1024]{3,0,2,1:T(8,128)S(1)} %fusion.39), kind=kOutput, calls=%fused_computation.39 | convolution fusion | flops 1880621056 | bytes 10747904 | tf_op jit(solution)/shard_map/pxmd,xdf->pxmf/dot_general | solution.py:36
  94.9 2.1 %fusion.18 = bf16[128,1,2,3584]{3,0,2,1:T(8,128)(2,1)S(1)} fusion(bf16[128,2,1024]{2,0,1:T(8,128)(2,1)S(1)} %fusion.79, bf16[1,1024,3584]{2,1,0:T(8,128)(2,1)S(1)} %bitcast.149), kind=kOutput, calls=%fused_computation.16 | convolution fusion | flops 1879965696 | bytes 9699328 | tf_op jit(solution)/shard_map/pxmf,xfd->pxmd/dot_general | solution.py:38
  97.0 3.1 %copy.23 = bf16[128,1,2,3584]{3,2,1,0:T(2,128)(2,1)} copy(bf16[128,1,2,3584]{3,0,2,1:T(8,128)(2,1)S(1)} %fusion.18) | data formatting | bytes 3670016 | tf_op jit(solution)/shard_map/convert_element_type | solution.py:38
  100.1 11.3 %all-to-all-done.1 = bf16[128,1,2,3584]{3,2,1,0:T(2,128)(2,1)S(1)} async-done(((bf16[128,1,2,3584]{3,2,1,0:T(2,128)(2,1)}), bf16[128,1,2,3584]{3,2,1,0:T(2,128)(2,1)S(1)}, u32[]{:S(2)}, u32[]{:S(2)}) %all-to-all-start.1) | async-done | bytes 1835040 | tf_op jit(solution)/shard_map/all_to_all | solution.py:54
  111.4 5.3 %all-to-all-start.3 = ((bf16[128,1,2,3584]{3,2,1,0:T(2,128)(2,1)}), bf16[128,1,2,3584]{3,2,1,0:T(2,128)(2,1)}, u32[]{:S(2)}, u32[]{:S(2)}) async-start(bf16[128,1,2,3584]{3,2,1,0:T(2,128)(2,1)} %copy.23), calls=%async_computation.3 | async-start | bytes 3670016 | tf_op jit(solution)/shard_map/all_to_all | solution.py:54
  117.5 1.6 %reshape.118 = bf16[256,3584]{1,0:T(8,128)(2,1)} reshape(bf16[128,1,2,3584]{3,2,1,0:T(2,128)(2,1)S(1)} %all-to-all-done.1) | data formatting | bytes 3670016 | tf_op jit(solution)/shard_map/reshape | solution.py:66
  119.1 2.3 %fusion.24 = bf16[8,1,3584]{2,0,1:T(8,128)(2,1)S(1)} fusion(f32[8,256]{1,0:T(8,128)S(1)} %fusion.93, bf16[256,3584]{1,0:T(8,128)(2,1)} %reshape.118), kind=kOutput, calls=%fused_computation.20 | convolution fusion | flops 88109056 | bytes 1900544 | tf_op jit(solution)/shard_map/dot_general | solution.py:67
  121.5 22.9 %all-to-all-done.3 = bf16[128,1,2,3584]{3,2,1,0:T(2,128)(2,1)} async-done(((bf16[128,1,2,3584]{3,2,1,0:T(2,128)(2,1)}), bf16[128,1,2,3584]{3,2,1,0:T(2,128)(2,1)}, u32[]{:S(2)}, u32[]{:S(2)}) %all-to-all-start.3) | async-done | bytes 1835040 | tf_op jit(solution)/shard_map/all_to_all | solution.py:54
  144.4 4.1 %reshape.122 = bf16[256,3584]{1,0:T(8,128)(2,1)S(1)} reshape(bf16[128,1,2,3584]{3,2,1,0:T(2,128)(2,1)} %all-to-all-done.3) | data formatting | bytes 3670016 | tf_op jit(solution)/shard_map/reshape | solution.py:66
  (37 shorter events, 5.9 us)
Async XLA Ops:
  6.4 39.4 %all-to-all-start = ((bf16[128,1,2,3584]{3,2,1,0:T(2,128)(2,1)}), bf16[128,1,2,3584]{3,2,1,0:T(2,128)(2,1)}, u32[]{:S(2)}, u32[]{:S(2)}) async-start(bf16[128,1,2,3584]{3,2,1,0:T(2,128)(2,1)} %bitcast.1), calls=%async_computation | async-start | bytes 3670016 | tf_op jit(solution)/shard_map/all_to_all | solution.py:56
  45.7 32.2 %all-to-all-start.2 = ((bf16[128,1,2,3584]{3,2,1,0:T(2,128)(2,1)}), bf16[128,1,2,3584]{3,2,1,0:T(2,128)(2,1)S(1)}, u32[]{:S(2)}, u32[]{:S(2)}) async-start(bf16[128,1,2,3584]{3,2,1,0:T(2,128)(2,1)} %bitcast.23), calls=%async_computation.2 | async-start | bytes 3670016 | tf_op jit(solution)/shard_map/all_to_all | solution.py:56
  50.0 11.9 %slice-start = ((s8[7340032]{0:T(1024)(128)(4,1)}), s8[4194304]{0:T(1024)(128)(4,1)S(1)}, s32[]{:S(2)}) async-start(s8[7340032]{0:T(1024)(128)(4,1)} %bitcast.146), calls=%async_computation.4 | async-start | bytes 8388608
  55.9 6.0 %slice-start.1 = ((s8[7340032]{0:T(1024)(128)(4,1)}), s8[3145728]{0:T(1024)(128)(4,1)S(1)}, s32[]{:S(2)}) async-start(s8[7340032]{0:T(1024)(128)(4,1)} %bitcast.146), calls=%async_computation.5 | async-start | bytes 6291456
  78.0 1.3 copy-start
  79.2 32.2 %all-to-all-start.1 = ((bf16[128,1,2,3584]{3,2,1,0:T(2,128)(2,1)}), bf16[128,1,2,3584]{3,2,1,0:T(2,128)(2,1)S(1)}, u32[]{:S(2)}, u32[]{:S(2)}) async-start(bf16[128,1,2,3584]{3,2,1,0:T(2,128)(2,1)} %copy.20), calls=%async_computation.1 | async-start | bytes 3670016 | tf_op jit(solution)/shard_map/all_to_all | solution.py:54
  83.5 5.9 %copy-start.1 = (bf16[128,1,2,3584]{3,2,1,0:T(2,128)(2,1)S(1)}, bf16[128,1,2,3584]{3,2,1,0:T(2,128)(2,1)}, u32[]{:S(2)}) copy-start(bf16[128,1,2,3584]{3,2,1,0:T(2,128)(2,1)} %copy-done) | copy-start | bytes 5505028
  83.5 11.3 %slice-start.2 = ((s8[7340032]{0:T(1024)(128)(4,1)}), s8[4194304]{0:T(1024)(128)(4,1)S(1)}, s32[]{:S(2)}) async-start(s8[7340032]{0:T(1024)(128)(4,1)} %bitcast.148), calls=%async_computation.6 | async-start | bytes 8388608
  89.4 5.5 %slice-start.3 = ((s8[7340032]{0:T(1024)(128)(4,1)}), s8[3145728]{0:T(1024)(128)(4,1)S(1)}, s32[]{:S(2)}) async-start(s8[7340032]{0:T(1024)(128)(4,1)} %bitcast.148), calls=%async_computation.7 | async-start | bytes 6291456
  100.1 16.6 %copy-start.2 = (f32[8,2,8]{2,1,0:T(2,128)S(1)}, f32[8,2,8]{2,1,0:T(2,128)}, u32[]{:S(2)}) copy-start(f32[8,2,8]{2,1,0:T(2,128)} %param.10) | copy-start | bytes 1540
  111.4 32.9 %all-to-all-start.3 = ((bf16[128,1,2,3584]{3,2,1,0:T(2,128)(2,1)}), bf16[128,1,2,3584]{3,2,1,0:T(2,128)(2,1)}, u32[]{:S(2)}, u32[]{:S(2)}) async-start(bf16[128,1,2,3584]{3,2,1,0:T(2,128)(2,1)} %copy.23), calls=%async_computation.3 | async-start | bytes 3670016 | tf_op jit(solution)/shard_map/all_to_all | solution.py:54
where the time goes:
time: 151 us; the launch traced here: 150 us
  waiting for transfers between devices  69.9 us (46%)
  matrix products  32.8 us (22%)
  starting transfers between devices  25.8 us (17%)
  local copies, waits for them, and re-layouts  18.5 us (12%)
  other arithmetic  2.78 us (2%)
    all_to_all x2, waiting for transfers between devices, mixture(): lax.all_to_all(shaped, ('grp', 'ep'), split_axis=0, concat_axis=0, tiled=...  35.7 us
    all_to_all x2, waiting for transfers between devices, mixture(): lax.all_to_all(run_experts(lax.all_to_all(shaped, ('grp', 'ep'), split_ax...  34.2 us
    all_to_all x2, starting transfers between devices, mixture(): lax.all_to_all(shaped, ('grp', 'ep'), split_axis=0, concat_axis=0, tiled=...  16.2 us
    dot_general x2, matrix products, run_experts(): jnp.einsum('pxmd,xdf->pxmf', arrived, w_gate, preferred_element_type=jnp....  11.7 us
    dot_general x2, matrix products, run_experts(): jnp.einsum('pxmd,xdf->pxmf', arrived, w_up, preferred_element_type=jnp.fl...  11.4 us
    all_to_all x2, starting transfers between devices, mixture(): lax.all_to_all(run_experts(lax.all_to_all(shaped, ('grp', 'ep'), split_ax...  9.63 us
    convert_element_type x2, local copies, waits for them, and re-layouts, run_experts(): jnp.einsum('pxmf,xfd->pxmd', act, w_down, preferred_element_type=jnp.floa...  6.26 us
    reshape x2, local copies, waits for them, and re-layouts, mixture(): flat_back = came_back.reshape(experts * most, dmodel).astype(jnp.float32)  5.7 us
  transfers between devices with their start and end apart: 4, of which 4 were waited for; matrix products, arithmetic and copies ran while one was open for 27% of the time, Pallas kernels for 0%

commit v1 on v0

v1 whole, which is shorter than its diff:
```python
import functools

import jax
import jax.numpy as jnp
from jax import lax
from jax.experimental import pallas as pl
from jax.experimental.pallas import tpu as pltpu
from jax.sharding import PartitionSpec as P

MESH = pl.DeviceIdType.MESH
F32 = jnp.float32
BF16 = jnp.bfloat16
ORDERS = (("y", "z", "x"), ("z", "x", "y"), ("x", "y", "z"))
STRIDE = {"x": 2, "y": 32, "z": 8}
RANGE = 4
ROWS = 16
META = 128


def part_widths(dmodel):
    tiles = dmodel // 256
    small = tiles // 3
    rest = tiles - small
    return (small * 256, rest // 2 * 256, (rest - rest // 2) * 256)


def device(coords):
    return (coords["y"], coords["z"] * 8 + coords["x"] * 2 + coords["core"])


def aligned(start, size):
    return pl.ds(pl.multiple_of(start, ROWS), size)


def iota(shape, dim):
    return lax.broadcasted_iota(jnp.int32, shape, dim)


def arrival_index(t, i):
    x, core, z, y, rank = i // 64, i // 32 % 2, i // 8 % 4, i // 2 % 4, i % 2
    at = {"x": x, "y": y, "z": z}
    a, b, c = ORDERS[t]
    return at[c] * 64 + core * 32 + at[b] * 8 + at[a] * 2 + rank


def kernel(
    widths,
    hid_ref,
    gain_ref,
    ig_ref,
    flat_ref,
    wg_hbm,
    wu_hbm,
    wd_hbm,
    out_ref,
    wg,
    wu,
    wd,
    xs,
    sb,
    ar,
    perm,
    perm_t,
    gates,
    gate_acc,
    up_acc,
    act,
    ob,
    bk,
    pb,
    r2,
    pb2,
    r1,
    w_sem,
    send_sem,
    p1_sem,
    p2a_sem,
    p2b_sem,
    p3_sem,
    own_sem,
    r3_sem,
    r2_sem,
    r1_sem,
):
    ep = lax.axis_index("ep")
    me = {"y": lax.axis_index("grp"), "z": ep // 8, "x": ep // 2 % 4, "core": ep % 2}
    offs = [sum(widths[:t]) for t in range(3)]

    def moved(axis, step, core=0):
        other = dict(me)
        other[axis] = (me[axis] + step) % RANGE
        other["core"] = (me["core"] + core) % 2
        return other

    barrier = pltpu.get_barrier_semaphore()
    partners = [moved(ax, s, c) for ax in "xyz" for s in (1, 2, 3) for c in (0, 1)] + [moved("x", 0, 1)]
    for other in partners:
        pl.semaphore_signal(barrier, inc=1, device_id=device(other), device_id_type=MESH)

    loads = [
        pltpu.make_async_copy(src.at[0], dst, w_sem.at[n])
        for n, (src, dst) in enumerate(((wg_hbm, wg), (wu_hbm, wu), (wd_hbm, wd)))
    ]
    for load in loads:
        load.start()

    hid = hid_ref[...].astype(F32)
    scale = lax.rsqrt(jnp.mean(hid * hid, axis=-1, keepdims=True) + 1e-06)
    normed = (hid * scale * gain_ref[...]).astype(BF16)

    ig = ig_ref[...]
    lane, row = iota((ROWS, META), 1), iota((ROWS, META), 0)
    before = lane // 8 < row
    meta = jnp.where(lane < 16, ig, 0.0)
    for k in range(8):
        same = jnp.where(before & (ig[:, k : k + 1] == flat_ref[...]), 1.0, 0.0)
        rank = jnp.sum(same, axis=1, keepdims=True)
        meta = jnp.where(lane == k, 2.0 * ig + rank, meta)
    meta = meta.astype(BF16)

    for t in range(3):
        a, b, _ = ORDERS[t]
        mine = aligned((me[b] * 4 + me[a]) * ROWS, ROWS)
        xs[t][mine, : widths[t]] = normed[:, offs[t] : offs[t] + widths[t]]
        xs[t][mine, widths[t] :] = meta

    pl.semaphore_wait(barrier, len(partners))

    sends = []

    def send(src, dst, sem, other):
        copy = pltpu.make_async_remote_copy(
            src, dst, send_sem, sem, device_id=device(other), device_id_type=MESH
        )
        copy.start()
        sends.append(copy)

    def arrive(ref, sem):
        pltpu.make_async_copy(ref, ref, sem).wait()

    for t in range(3):
        a, b, _ = ORDERS[t]
        mine = xs[t].at[aligned((me[b] * 4 + me[a]) * ROWS, ROWS)]
        for step in (1, 3, 2):
            send(mine, mine, p1_sem.at[t], moved(a, step))

    for t in (1, 2):
        i, j = iota((256, 256), 0), iota((256, 256), 1)
        perm[t - 1] = jnp.where(arrival_index(t, i) == j, 1.0, 0.0).astype(BF16)
        perm_t[t - 1] = jnp.where(arrival_index(t, j) == i, 1.0, 0.0).astype(BF16)

    for t in range(3):
        a, b, _ = ORDERS[t]
        arrive(xs[t].at[pl.ds(0, 3 * ROWS)], p1_sem.at[t])
        mine = xs[t].at[aligned(me[b] * 64, 64)]
        pair = dict(me)
        pair[b] = me[b] + 1 - 2 * (me[b] % 2)
        send(mine, mine, p2a_sem.at[t], pair)
        across = dict(me)
        across[b] = (pair[b] + 2) % RANGE
        send(mine, mine, p2b_sem.at[t], across)
        send(mine, mine, p2b_sem.at[t], moved(b, 2))

    def slots(t, half):
        _, _, c = ORDERS[t]
        base = dict(me)
        base[c] = 0
        first = base["y"] * 32 + base["z"] * 8 + base["x"] * 2
        rows = aligned(half * 128, 128)
        info = xs[t][rows, widths[t] :].astype(F32).T
        i, j = iota((128, 128), 0), iota((128, 128), 1)
        expert = first + i // 32 * STRIDE[c] + i // 16 % 2
        code = (expert * 2 + i % 2).astype(F32)
        hit = jnp.zeros((128, 128), F32)
        for k in range(8):
            hit = jnp.where(info[k : k + 1, :] == code, 1.0, hit)
        hit = jnp.where(j // 16 == i % 16 // 2, hit, 0.0).astype(BF16)
        sb[t][half] = jnp.dot(hit, xs[t][rows, : widths[t]], preferred_element_type=F32).astype(BF16)
        spot = me[c] * 2 + me["core"]
        there = ar[t].at[aligned(spot * 32 + half * 16, 16)]
        for step in (1, 3, 2, 0):
            for core in (0, 1):
                other = moved(c, step, core)
                piece = sb[t].at[half, aligned((other[c] * 2 + other["core"]) * 16, 16)]
                if step == 0 and core == 0:
                    pltpu.make_async_copy(piece, there, own_sem.at[t]).start()
                else:
                    send(piece, there, p3_sem.at[t], other)

    for t in range(3):
        b = ORDERS[t][1]
        arrive(xs[t].at[pl.ds(0, 64)], p2a_sem.at[t])
        slots(t, me[b] // 2)
    for t in range(3):
        b = ORDERS[t][1]
        arrive(xs[t].at[pl.ds(0, 128)], p2b_sem.at[t])
        slots(t, 1 - me[b] // 2)

    for t in range(3):
        _, _, c = ORDERS[t]
        base = dict(me)
        base[c] = 0
        first = base["y"] * 32 + base["z"] * 8 + base["x"] * 2
        l = iota((64, 256), 1)
        code = ((first + l // 64 * STRIDE[c] + l // 32 % 2) * 2 + l % 2).astype(F32)
        for q in range(4):
            info = xs[t][q * 64 : (q + 1) * 64, widths[t] :].astype(F32)
            owner = q * 4 + iota((64, 256), 0) // 16
            weight = jnp.zeros((64, 256), F32)
            for k in range(8):
                weight = jnp.where(info[:, k : k + 1] == code, info[:, 8 + k : 9 + k], weight)
            weight = jnp.where(owner == l % 32 // 2, weight, 0.0)
            gates[t, q * 64 : (q + 1) * 64] = weight.astype(BF16)

    loads[0].wait()
    loads[1].wait()
    hidden_units = gate_acc.shape[1]
    for t in range(3):
        for _ in range(2):
            arrive(ar[t].at[pl.ds(0, 16)], own_sem.at[t])
        arrive(ar[t].at[pl.ds(0, 224)], p3_sem.at[t])
        if t > 0:
            ar[t][...] = jnp.dot(perm[t - 1], ar[t][...], preferred_element_type=F32).astype(BF16)
        depth = pl.ds(offs[t], widths[t])

        def tile(n, carry, t=t, depth=depth):
            cols = pl.ds(pl.multiple_of(n * 256, 256), 256)
            for weights, total in ((wg, gate_acc), (wu, up_acc)):
                part = jnp.dot(ar[t][...], weights[depth, cols], preferred_element_type=F32)
                total[:, cols] = part if t == 0 else total[:, cols] + part
            return carry

        lax.fori_loop(0, hidden_units // 256, tile, 0)

    gate = gate_acc[...]
    act[0] = (gate / (1.0 + jnp.exp(-gate)) * up_acc[...]).astype(BF16)

    loads[2].wait()
    for t in range(3):
        _, _, c = ORDERS[t]
        if t > 0:
            act[t] = jnp.dot(perm_t[t - 1], act[0], preferred_element_type=F32).astype(BF16)

        def tile(n, carry, t=t):
            cols = pl.ds(pl.multiple_of(n * 256, 256), 256)
            from_cols = pl.ds(pl.multiple_of(offs[t] + n * 256, 256), 256)
            ob[t][:, cols] = jnp.dot(act[t], wd[:, from_cols], preferred_element_type=F32).astype(BF16)
            return carry

        lax.fori_loop(0, widths[t] // 256, tile, 0)
        spot = me[c] * 2 + me["core"]
        there = bk[t].at[aligned(spot * 32, 32)]
        for step in (1, 3, 2, 0):
            for core in (0, 1):
                other = moved(c, step, core)
                piece = ob[t].at[aligned((other[c] * 2 + other["core"]) * 32, 32)]
                if step == 0 and core == 0:
                    pltpu.make_async_copy(piece, there, own_sem.at[t]).start()
                else:
                    send(piece, there, r3_sem.at[t], other)

    for t in range(3):
        _, b, _ = ORDERS[t]
        arrive(bk[t].at[pl.ds(0, 32)], own_sem.at[t])
        arrive(bk[t].at[pl.ds(0, 224)], r3_sem.at[t])
        pb[t][...] = jnp.dot(gates[t], bk[t][...], preferred_element_type=F32).astype(BF16)
        there = r2[t].at[aligned(me[b] * 64, 64)]
        for step in (1, 3, 2):
            other = moved(b, step)
            send(pb[t].at[aligned(other[b] * 64, 64)], there, r2_sem.at[t], other)
        mine = aligned(me[b] * 64, 64)
        r2[t][mine] = pb[t][mine]

    for t in range(3):
        a, _, _ = ORDERS[t]
        arrive(r2[t].at[pl.ds(0, 192)], r2_sem.at[t])
        total = r2[t][0:64].astype(F32)
        for n in range(1, 4):
            total = total + r2[t][n * 64 : (n + 1) * 64].astype(F32)
        pb2[t][...] = total.astype(BF16)
        there = r1[t].at[aligned(me[a] * 16, 16)]
        for step in (1, 3, 2):
            other = moved(a, step)
            send(pb2[t].at[aligned(other[a] * 16, 16)], there, r1_sem.at[t], other)
        mine = aligned(me[a] * 16, 16)
        r1[t][mine] = pb2[t][mine]

    for t in range(3):
        arrive(r1[t].at[pl.ds(0, 48)], r1_sem.at[t])
        total = r1[t][0:16].astype(F32)
        for n in range(1, 4):
            total = total + r1[t][n * 16 : (n + 1) * 16].astype(F32)
        out_ref[:, offs[t] : offs[t] + widths[t]] = total.astype(BF16)

    for copy in sends:
        copy.wait_send()


def body(hidden, norm_gain, route_ids, gate_weights, w_gate, w_up, w_down):
    rows, steps, dmodel = hidden.shape
    topk = route_ids.shape[2]
    units = w_gate.shape[2]
    widths = part_widths(dmodel)
    count = rows * steps
    ids = route_ids.reshape(count, topk).astype(F32)
    ig = jnp.concatenate([ids, gate_weights.reshape(count, topk)], axis=1)
    ig = jnp.pad(ig, ((0, 0), (0, META - 2 * topk)))

    def each(rows_of, extra=0):
        return [pltpu.VMEM((*rows_of, w + extra), BF16) for w in widths]

    vmem = pl.BlockSpec(memory_space=pltpu.VMEM)
    hbm = pl.BlockSpec(memory_space=pl.ANY)
    sem = pltpu.SemaphoreType.DMA
    result = pl.pallas_call(
        functools.partial(kernel, widths),
        out_shape=jax.ShapeDtypeStruct((count, dmodel), BF16),
        in_specs=[vmem] * 4 + [hbm] * 3,
        out_specs=vmem,
        scratch_shapes=[
            pltpu.VMEM((dmodel, units), BF16),
            pltpu.VMEM((dmodel, units), BF16),
            pltpu.VMEM((units, dmodel), BF16),
            each((256,), META),
            each((2, 128)),
            each((256,)),
            pltpu.VMEM((2, 256, 256), BF16),
            pltpu.VMEM((2, 256, 256), BF16),
            pltpu.VMEM((3, 256, 256), BF16),
            pltpu.VMEM((256, units), F32),
            pltpu.VMEM((256, units), F32),
            pltpu.VMEM((3, 256, units), BF16),
            each((256,)),
            each((256,)),
            each((256,)),
            each((256,)),
            each((64,)),
            each((64,)),
            sem((3,)),
            sem,
            sem((3,)),
            sem((3,)),
            sem((3,)),
            sem((3,)),
            sem((3,)),
            sem((3,)),
            sem((3,)),
            sem((3,)),
        ],
        compiler_params=pltpu.CompilerParams(
            collective_id=0, has_side_effects=True, vmem_limit_bytes=56 * 2**20
        ),
        cost_estimate=pl.CostEstimate(
            flops=6 * 256 * dmodel * units, bytes_accessed=6 * dmodel * units, transcendentals=256 * units
        ),
    )(
        hidden.reshape(count, dmodel),
        norm_gain.reshape(1, dmodel),
        ig,
        ids.reshape(1, count * topk),
        w_gate,
        w_up,
        w_down,
    )
    return result.reshape(rows, steps, dmodel)


def solution(mesh):
    split = P(("grp", "ep"), None, None)
    return jax.shard_map(
        body,
        mesh=mesh,
        in_specs=(split, P(), split, split, split, split, split),
        out_specs=split,
        check_vma=False,
    )
```

time: 151 us -> 72.4 us (0.48)
  waiting for transfers between devices: 69.9 us -> 0 us
  Pallas kernels: 0 us -> 64.3 us
  matrix products: 32.8 us -> 0 us
  starting transfers between devices: 25.8 us -> 0 us
  local copies, waits for them, and re-layouts: 18.5 us -> 5.18 us
    all_to_all x4 -> x0, waiting for transfers between devices: 69.9 us -> none  [the longest x2 35.7 us: mixture(): lax.all_to_all(shaped, ('grp', 'ep'), split_axis=0, concat_axis=0, tiled=...]
    pallas_call x0 -> x1, Pallas kernels: none -> 64.3 us  [body(): pl.pallas_call(functools.partial(kernel, widths), out_shape=jax.ShapeDtyp...]
    dot_general x12 -> x0, matrix products: 32.8 us -> none  [the longest x2 11.7 us: run_experts(): jnp.einsum('pxmd,xdf->pxmf', arrived, w_gate, preferred_element_type=jnp....]
    all_to_all x4 -> x0, starting transfers between devices: 25.8 us -> none  [the longest x2 16.2 us: mixture(): lax.all_to_all(shaped, ('grp', 'ep'), split_axis=0, concat_axis=0, tiled=...]
    convert_element_type x2 -> x1, local copies, waits for them, and re-layouts: 6.26 us -> 0.68 us  [body(): ids = route_ids.reshape(count, topk).astype(F32)]
    reshape x4 -> x3, local copies, waits for them, and re-layouts: 9.04 us -> 4.51 us  [the longest x1 1.59 us: body(): return result.reshape(rows, steps, dmodel)]
  transfers between devices with their start and end apart: 4 -> 0, of which waited for: 4 -> 0; matrix products, arithmetic and copies ran while one was open for 27% -> 0% of each run, Pallas kernels for 0% -> 0%
where the time goes in v1:
time: 72.4 us; the launch traced here: 71.6 us
  Pallas kernels  64.3 us (89%)
  local copies, waits for them, and re-layouts  5.18 us (7%)
  other arithmetic  2.07 us (3%)
    pallas_call x1, Pallas kernels, body(): pl.pallas_call(functools.partial(kernel, widths), out_shape=jax.ShapeDtyp...  64.3 us
    reshape x1, local copies, waits for them, and re-layouts, body(): return result.reshape(rows, steps, dmodel)  1.59 us
    reshape x1, local copies, waits for them, and re-layouts, body(): hidden.reshape(count, dmodel)  1.59 us

profile of v1, /device:TPU:1, one launch (start us, length us, event | category | flops | bytes accessed | tf_op | source)
XLA Modules:
  0.0 71.6 jit_solution(8180199214651835508)
XLA Ops:
  0.0 0.7 convert_element_type.18
  0.7 0.7 convert_element_type.20.flat_ref
  1.4 1.4 %select_maximum_fusion.ig_ref = f32[16,128]{1,0:T(8,128)} fusion(f32[16,8]{1,0:T(8,128)} %bitcast.3, f32[16,8]{1,0:T(8,128)S(1)} %bitcast.2), kind=kLoop, calls=%fused_computation | loop fusion | flops 8192 | bytes 9216 | tf_op jit(solution)/shard_map/concatenate | solution.py:306
  2.7 1.3 %reshape.27.gain_ref = f32[1,3584]{1,0:T(1,128)} reshape(f32[3584]{0:T(1024)} %param.8) | data formatting | bytes 28672 | tf_op jit(solution)/shard_map/reshape | solution.py:358
  4.1 1.6 %reshape.26.hid_ref = bf16[16,3584]{1,0:T(8,128)(2,1)} reshape(bf16[8,2,3584]{2,1,0:T(2,128)(2,1)} %param.7) | data formatting | bytes 229376 | tf_op jit(solution)/shard_map/reshape | solution.py:357
  5.7 64.3 %shard_map.73 = bf16[16,3584]{1,0:T(8,128)(2,1)} custom-call(bf16[16,3584]{1,0:T(8,128)(2,1)} %reshape.26.hid_ref, f32[1,3584]{1,0:T(1,128)} %reshape.27.gain_ref, f32[16,128]{1,0:T(8,128)} %select_maximum_fusion.ig_ref, f32[1,128]{1,0:T(1,128)} %convert_element_type.20.flat_ref, bf16[1,3584,1024]{2,1,0:T(8,128)(2,1)} %wg_hbm.1, ...), custom_call_target="tpu_custom_call" | custom-call | flops 5637144576 | bytes 22020096 | tf_op jit(solution)/shard_map/pallas_call | solution.py:315
  70.0 1.6 %reshape.29 = bf16[8,2,3584]{2,1,0:T(2,128)(2,1)} reshape(bf16[16,3584]{1,0:T(8,128)(2,1)} %shard_map.73) | data formatting | bytes 229376 | tf_op jit(solution)/shard_map/reshape | solution.py:365

commit v2 on v1

v2 whole, which is shorter than its diff:
```python
import functools

import jax
import jax.numpy as jnp
from jax import lax
from jax.experimental import pallas as pl
from jax.experimental.pallas import tpu as pltpu
from jax.sharding import PartitionSpec as P

MESH = pl.DeviceIdType.MESH
F32 = jnp.float32
BF16 = jnp.bfloat16
ORDERS = (("y", "z", "x"), ("z", "x", "y"), ("x", "y", "z"))
STRIDE = {"x": 2, "y": 32, "z": 8}
RANGE = 4
ROWS = 16
META = 128
PLANE = 32
SLOTS = 8
UNITS = 2


PEERS = [(i, j, core) for i in (2, 1, 3, 0) for j in (2, 1, 3, 0) for core in (1, 0)][:-1]


def part_widths(dmodel):
    tiles, count = dmodel // 256, 3 * UNITS
    width = [tiles // count] * count
    for n in range(tiles % count):
        width[(n * 2 + n // 3) % count if UNITS > 1 else n] += 1
    return tuple(w * 256 for w in width)


def device(coords):
    return (coords["y"], coords["z"] * 8 + coords["x"] * 2 + coords["core"])


def aligned(start, size):
    return pl.ds(pl.multiple_of(start, ROWS), size)


def iota(shape, dim):
    return lax.broadcasted_iota(jnp.int32, shape, dim)


def arrival_index(t, i):
    z, x, core, y, rank = i // 64, i // 16 % 4, i // 8 % 2, i // 2 % 4, i % 2
    at = {"x": x, "y": y, "z": z}
    a, b, c = ORDERS[t]
    return at[b] * 64 + at[c] * 16 + core * 8 + at[a] * 2 + rank


def kernel(
    widths,
    hid_ref,
    gain_ref,
    ids_ref,
    gw_ref,
    wg_hbm,
    wu_hbm,
    wd_hbm,
    out_ref,
    wg,
    wu,
    wd,
    xs,
    sb,
    ar,
    perm,
    perm_t,
    hits_of,
    gates,
    gate_acc,
    up_acc,
    act,
    ob,
    bk,
    pf,
    pb,
    r1,
    w_sem,
    send_sem,
    p1_sem,
    p2_sem,
    r2_sem,
    r1_sem,
):
    ep = lax.axis_index("ep")
    me = {"y": lax.axis_index("grp"), "z": ep // 8, "x": ep // 2 % 4, "core": ep % 2}
    chunks = range(len(widths))
    offs = [sum(widths[:n]) for n in chunks]

    def moved(steps):
        other = dict(me)
        for axis, step in steps.items():
            other[axis] = (me[axis] + step) % (2 if axis == "core" else RANGE)
        return other

    barrier = pltpu.get_barrier_semaphore()
    steps = [
        {"x": x, "y": y, "z": z, "core": core}
        for x in range(4)
        for y in range(4)
        for z in range(4)
        for core in range(2)
        if (x, y, z).count(0) >= 2 and (x, y, z, core) != (0, 0, 0, 0)
    ]
    for step in steps:
        pl.semaphore_signal(barrier, inc=1, device_id=device(moved(step)), device_id_type=MESH)

    loads = [
        pltpu.make_async_copy(src.at[0], dst, w_sem.at[n])
        for n, (src, dst) in enumerate(((wg_hbm, wg), (wu_hbm, wu), (wd_hbm, wd)))
    ]
    for load in loads:
        load.start()

    hid = hid_ref[...].astype(F32).reshape(ROWS, hid_ref.shape[2])
    scale = lax.rsqrt(jnp.mean(hid * hid, axis=-1, keepdims=True) + 1e-06)
    normed = (hid * scale * gain_ref[...].reshape(1, gain_ref.shape[0])).astype(BF16)

    topk = ids_ref.shape[2]
    ids = ids_ref[...].astype(F32).reshape(ROWS, topk)
    gw = gw_ref[...].reshape(ROWS, topk)
    lane = iota((ROWS, META), 1)
    lane_f = lane.astype(F32)
    hits = jnp.zeros((ROWS, META), F32)
    for k in range(topk):
        hits = jnp.where(ids[:, k : k + 1] == lane_f, 1.0, hits)
    lower = jnp.where(iota((ROWS, ROWS), 1) < iota((ROWS, ROWS), 0), 1.0, 0.0).astype(BF16)
    earlier = jnp.dot(lower, hits.astype(BF16), preferred_element_type=F32)
    meta = jnp.zeros((ROWS, META), F32)
    for k in range(topk):
        own = ids[:, k : k + 1]
        rank = jnp.sum(jnp.where(own == lane_f, earlier, 0.0), axis=1, keepdims=True)
        meta = jnp.where(lane == k, 2.0 * own + rank, meta)
        meta = jnp.where(lane == topk + k, gw[:, k : k + 1], meta)
    meta = meta.astype(BF16)

    for n in chunks:
        mine = aligned(me[ORDERS[n % 3][0]] * ROWS, ROWS)
        xs[n][mine, : widths[n]] = normed[:, offs[n] : offs[n] + widths[n]]
        if n < 3:
            xs[n][mine, widths[n] :] = meta

    pl.semaphore_wait(barrier, len(steps))

    sends = []

    def send(src, dst, sem, other):
        copy = pltpu.make_async_remote_copy(
            src, dst, send_sem, sem, device_id=device(other), device_id_type=MESH
        )
        copy.start()
        sends.append(copy)

    def arrive(ref, sem):
        pltpu.make_async_copy(ref, ref, sem).wait()

    def place(t, coords):
        _, b, c = ORDERS[t]
        return coords[b] * 8 + coords[c] * 2 + coords["core"]

    def over_planes(first, src, dst, sem):
        for s0, s1, core in PEERS:
            for n in (first, first + 1, first + 2):
                _, b, c = ORDERS[n % 3]
                other = moved({b: s0, c: s1, "core": core})
                send(src[n].at[place(n % 3, other)], dst[n].at[place(n % 3, me)], sem.at[n], other)
        for n in (first, first + 1, first + 2):
            here = place(n % 3, me)
            dst[n][here] = src[n][here]

    for n in chunks:
        a = ORDERS[n % 3][0]
        mine = xs[n].at[aligned(me[a] * ROWS, ROWS)]
        for step in (1, 3, 2):
            send(mine, mine, p1_sem.at[n], moved({a: step}))

    for t in (1, 2):
        i, j = iota((256, 256), 0), iota((256, 256), 1)
        perm[t - 1] = jnp.where(arrival_index(t, i) == j, 1.0, 0.0).astype(BF16)
        perm_t[t - 1] = jnp.where(arrival_index(t, j) == i, 1.0, 0.0).astype(BF16)

    def slot_code(t, slot):
        _, b, c = ORDERS[t]
        base = dict(me)
        base[b], base[c] = 0, 0
        first = base["y"] * 32 + base["z"] * 8 + base["x"] * 2
        expert = first + slot // 64 * STRIDE[b] + slot // 16 % 4 * STRIDE[c] + slot // 8 % 2
        return (expert * 2 + slot % 2).astype(F32)

    for t in range(3):
        arrive(xs[t].at[pl.ds(0, 3 * ROWS)], p1_sem.at[t])
    for n in chunks:
        t = n % 3
        if n < 3:
            info = xs[t][:, widths[t] :].astype(F32).T
            slot, row = iota((256, 64), 0), iota((256, 64), 1)
            code = slot_code(t, slot)
            hit = jnp.zeros((256, 64), F32)
            for k in range(topk):
                hit = jnp.where(info[k : k + 1, :] == code, 1.0, hit)
            hits_of[t] = jnp.where(row // ROWS == slot % 8 // 2, hit, 0.0).astype(BF16)
        else:
            arrive(xs[n].at[pl.ds(0, 3 * ROWS)], p1_sem.at[n])
        picked = jnp.dot(hits_of[t], xs[n][:, : widths[n]], preferred_element_type=F32).astype(BF16)
        sb[n][...] = picked.reshape(PLANE, SLOTS, widths[n])
        if t == 2:
            over_planes(n - 2, sb, ar, p2_sem)

    for t in range(3):
        info = xs[t][:, widths[t] :].astype(F32)
        row, slot = iota((64, 256), 0), iota((64, 256), 1)
        code = slot_code(t, slot)
        weight = jnp.zeros((64, 256), F32)
        for k in range(topk):
            weight = jnp.where(info[:, k : k + 1] == code, info[:, topk + k : topk + k + 1], weight)
        gates[t] = jnp.where(row // ROWS == slot % 8 // 2, weight, 0.0).astype(BF16)

    loads[0].wait()
    loads[1].wait()
    units = gate_acc.shape[1]
    for n in chunks:
        arrive(ar[n].at[pl.ds(0, PLANE - 1)], p2_sem.at[n])
        rows = ar[n][...].reshape(PLANE * SLOTS, widths[n])
        if n % 3 > 0:
            rows = jnp.dot(perm[n % 3 - 1], rows, preferred_element_type=F32).astype(BF16)
        depth = pl.ds(offs[n], widths[n])
        for first in range(0, units, 512):
            cols = pl.ds(first, 512)
            for weights, total in ((wg, gate_acc), (wu, up_acc)):
                part = jnp.dot(rows, weights[depth, cols], preferred_element_type=F32)
                total[:, cols] = part if n == 0 else total[:, cols] + part

    gate = gate_acc[...]
    act[0] = (gate / (1.0 + jnp.exp(-gate)) * up_acc[...]).astype(BF16)

    loads[2].wait()
    for n in chunks:
        t = n % 3
        if n in (1, 2):
            act[t] = jnp.dot(perm_t[t - 1], act[0], preferred_element_type=F32).astype(BF16)
        for first in range(0, widths[n], 256):
            cols = pl.ds(offs[n] + first, 256)
            made = jnp.dot(act[t], wd[:, cols], preferred_element_type=F32).astype(BF16)
            ob[n][:, :, first : first + 256] = made.reshape(PLANE, SLOTS, 256)
        if t == 2:
            over_planes(n - 2, ob, bk, r2_sem)

    for n in chunks:
        a = ORDERS[n % 3][0]
        arrive(bk[n].at[pl.ds(0, PLANE - 1)], r2_sem.at[n])
        back = bk[n][...].reshape(PLANE * SLOTS, widths[n])
        pf[n][...] = jnp.dot(gates[n % 3], back, preferred_element_type=F32)
        pb[n][...] = pf[n][...].astype(BF16)
        there = r1[n].at[aligned(me[a] * ROWS, ROWS)]
        for step in (1, 3, 2):
            other = moved({a: step})
            send(pb[n].at[aligned(other[a] * ROWS, ROWS)], there, r1_sem.at[n], other)
        r1[n][aligned(me[a] * ROWS, ROWS)] = jnp.zeros((ROWS, widths[n]), BF16)

    for n in chunks:
        a = ORDERS[n % 3][0]
        arrive(r1[n].at[pl.ds(0, 3 * ROWS)], r1_sem.at[n])
        total = pf[n][aligned(me[a] * ROWS, ROWS)]
        for k in range(4):
            total = total + r1[n][k * ROWS : (k + 1) * ROWS].astype(F32)
        out_ref[:, :, offs[n] : offs[n] + widths[n]] = total.reshape(ROWS // 2, 2, widths[n]).astype(BF16)

    for copy in sends:
        copy.wait_send()


def body(hidden, norm_gain, route_ids, gate_weights, w_gate, w_up, w_down):
    rows, steps, dmodel = hidden.shape
    topk = route_ids.shape[2]
    units = w_gate.shape[2]
    widths = part_widths(dmodel)
    count = rows * steps

    def each(rows_of, extra=0, kind=BF16):
        return [pltpu.VMEM((*rows_of, w + extra * (n < 3)), kind) for n, w in enumerate(widths)]

    vmem = pl.BlockSpec(memory_space=pltpu.VMEM)
    hbm = pl.BlockSpec(memory_space=pl.ANY)
    sem = pltpu.SemaphoreType.DMA
    result = pl.pallas_call(
        functools.partial(kernel, widths),
        out_shape=jax.ShapeDtypeStruct(hidden.shape, BF16),
        in_specs=[vmem] * 4 + [hbm] * 3,
        out_specs=vmem,
        scratch_shapes=[
            pltpu.VMEM((dmodel, units), BF16),
            pltpu.VMEM((dmodel, units), BF16),
            pltpu.VMEM((units, dmodel), BF16),
            each((64,), META),
            each((PLANE, SLOTS)),
            each((PLANE, SLOTS)),
            pltpu.VMEM((2, 256, 256), BF16),
            pltpu.VMEM((2, 256, 256), BF16),
            pltpu.VMEM((3, 256, 64), BF16),
            pltpu.VMEM((3, 64, 256), BF16),
            pltpu.VMEM((256, units), F32),
            pltpu.VMEM((256, units), F32),
            pltpu.VMEM((3, 256, units), BF16),
            each((PLANE, SLOTS)),
            each((PLANE, SLOTS)),
            each((64,), kind=F32),
            each((64,)),
            each((64,)),
            sem((3,)),
            sem,
        ]
        + [sem((len(widths),))] * 4,
        compiler_params=pltpu.CompilerParams(
            collective_id=0, has_side_effects=True, vmem_limit_bytes=56 * 2**20
        ),
        cost_estimate=pl.CostEstimate(
            flops=6 * 256 * dmodel * units, bytes_accessed=6 * dmodel * units, transcendentals=256 * units
        ),
    )(
        hidden,
        norm_gain,
        route_ids,
        gate_weights,
        w_gate,
        w_up,
        w_down,
    )
    return result


def solution(mesh):
    split = P(("grp", "ep"), None, None)
    return jax.shard_map(
        body,
        mesh=mesh,
        in_specs=(split, P(), split, split, split, split, split),
        out_specs=split,
        check_vma=False,
    )
```

time: 72.4 us -> 56.3 us (0.78)
  Pallas kernels: 64.3 us -> 54.5 us
  local copies, waits for them, and re-layouts: 5.18 us -> 1.62 us
  other arithmetic: 2.07 us -> 0 us
    pallas_call x1, Pallas kernels: 64.3 us -> 54.5 us  [body(): pl.pallas_call(functools.partial(kernel, widths), out_shape=jax.ShapeDtyp...]
    reshape x3 -> x0, local copies, waits for them, and re-layouts: 4.51 us -> none  [the longest x1 1.59 us: body(): return result.reshape(rows, steps, dmodel)]
    unnamed x0 -> x1, local copies, waits for them, and re-layouts: none -> 1.62 us
    concatenate x1 -> x0, other arithmetic: 1.37 us -> none  [body(): ig = jnp.concatenate([ids, gate_weights.reshape(count, topk)], axis=1)]
where the time goes in v2:
time: 56.3 us; the launch traced here: 56.1 us
  Pallas kernels  54.5 us (97%)
  local copies, waits for them, and re-layouts  1.62 us (3%)
    pallas_call x1, Pallas kernels, body(): pl.pallas_call(functools.partial(kernel, widths), out_shape=jax.ShapeDtyp...  54.5 us
    unnamed x1, local copies, waits for them, and re-layouts  1.62 us

profile of v2, /device:TPU:1, one launch (start us, length us, event | category | flops | bytes accessed | tf_op | source)
XLA Modules:
  0.0 56.1 jit_solution(3562672015351106506)
XLA Ops:
  0.0 54.5 %shard_map.73 = bf16[8,2,3584]{2,1,0:T(2,128)(2,1)} custom-call(bf16[8,2,3584]{2,1,0:T(2,128)(2,1)} %hid_ref.1, f32[3584]{0:T(1024)} %gain_ref.1, s32[8,2,8]{2,1,0:T(2,128)} %ids_ref.1, f32[8,2,8]{2,1,0:T(2,128)} %gw_ref.1, bf16[1,3584,1024]{2,1,0:T(8,128)(2,1)} %wg_hbm.1, bf16[1,3584,1024]{2,1,0:T(8,128)(2,1)} %wu_hbm.1, bf16[1,1024,3584]{2,1,0:T(8,128)(2,1)} %wd_hbm.1), custom_call_target="tpu_custom_call" | custom-call | flops 5637144576 | bytes 22020096 | tf_op jit(solution)/shard_map/pallas_call | solution.py:288
  54.5 1.6 %copy.9 = bf16[8,2,3584]{2,1,0:T(2,128)(2,1)} copy(bf16[8,2,3584]{2,1,0:T(2,128)(2,1)} %shard_map.73) | data formatting | bytes 229376

commit v3 on v2

v3 whole, which is shorter than its diff:
```python
import functools

import jax
import jax.numpy as jnp
from jax import lax
from jax.experimental import pallas as pl
from jax.experimental.pallas import tpu as pltpu
from jax.sharding import PartitionSpec as P

MESH = pl.DeviceIdType.MESH
F32 = jnp.float32
BF16 = jnp.bfloat16
ORDERS = (("y", "z", "x"), ("z", "x", "y"), ("x", "y", "z"))
STRIDE = {"x": 2, "y": 32, "z": 8}
RANGE = 4
ROWS = 16
META = 128
PLANE = 16
SLOTS = 8
HALF = PLANE * SLOTS
PEERS = [(i, j) for i in (2, 1, 3, 0) for j in (2, 1, 3, 0)]


def part_widths(dmodel):
    tiles = dmodel // 128
    small = tiles // 3
    rest = tiles - small
    return ((rest - rest // 2) * 128, rest // 2 * 128, small * 128)


def device(coords):
    return (coords["y"], coords["z"] * 8 + coords["x"] * 2 + coords["core"])


def aligned(start, size):
    return pl.ds(pl.multiple_of(start, ROWS), size)


def iota(shape, dim):
    return lax.broadcasted_iota(jnp.int32, shape, dim)


def arrival_index(t, i):
    z, x, y, rank = i // 32, i // 8 % 4, i // 2 % 4, i % 2
    at = {"x": x, "y": y, "z": z}
    a, b, c = ORDERS[t]
    return at[b] * 32 + at[c] * 8 + at[a] * 2 + rank


def kernel(
    widths,
    hid_hbm,
    gain_hbm,
    ids_hbm,
    gw_hbm,
    wg_hbm,
    wu_hbm,
    wd_hbm,
    out_hbm,
    hid_ref,
    gain_ref,
    ids_ref,
    gw_ref,
    out_ref,
    wg,
    wu,
    wd,
    xs,
    sb,
    ar,
    perm,
    perm_t,
    gates,
    gate_acc,
    up_acc,
    act,
    ob,
    bk,
    pf,
    pb,
    r1,
    io_sem,
    w_sem,
    send_sem,
    p1_sem,
    p2_sem,
    r2_sem,
    r1_sem,
):
    ep = lax.axis_index("ep")
    me = {"y": lax.axis_index("grp"), "z": ep // 8, "x": ep // 2 % 4, "core": ep % 2}
    parts = range(3)
    offs = [sum(widths[:t]) for t in parts]

    def moved(steps):
        other = dict(me)
        for axis, step in steps.items():
            other[axis] = (me[axis] + step) % (2 if axis == "core" else RANGE)
        return other

    barrier = pltpu.get_barrier_semaphore()
    steps = [
        {"x": x, "y": y, "z": z, "core": core}
        for x in range(4)
        for y in range(4)
        for z in range(4)
        for core in range(2)
        if (x, y, z).count(0) >= 2 and (x, y, z, core) != (0, 0, 0, 0)
    ]
    for step in steps:
        pl.semaphore_signal(barrier, inc=1, device_id=device(moved(step)), device_id_type=MESH)

    inputs = [
        pltpu.make_async_copy(src, dst, io_sem.at[n])
        for n, (src, dst) in enumerate(
            ((hid_hbm, hid_ref), (gain_hbm, gain_ref), (ids_hbm, ids_ref), (gw_hbm, gw_ref))
        )
    ]
    for load in inputs:
        load.start()

    loads = [
        pltpu.make_async_copy(src.at[0], dst, w_sem.at[n])
        for n, (src, dst) in enumerate(((wg_hbm, wg), (wu_hbm, wu), (wd_hbm, wd)))
    ]
    for load in inputs:
        load.wait()
    for load in loads:
        load.start()
    hid = hid_ref[...].astype(F32).reshape(ROWS, hid_ref.shape[2])
    scale = lax.rsqrt(jnp.mean(hid * hid, axis=-1, keepdims=True) + 1e-06)
    normed = (hid * scale * gain_ref[...].reshape(1, gain_ref.shape[0])).astype(BF16)

    topk = ids_ref.shape[2]
    ids = ids_ref[...].astype(F32).reshape(ROWS, topk)
    gw = gw_ref[...].reshape(ROWS, topk)
    lane = iota((ROWS, META), 1)
    lane_f = lane.astype(F32)
    hits = jnp.zeros((ROWS, META), F32)
    for k in range(topk):
        hits = jnp.where(ids[:, k : k + 1] == lane_f, 1.0, hits)
    lower = jnp.where(iota((ROWS, ROWS), 1) < iota((ROWS, ROWS), 0), 1.0, 0.0).astype(BF16)
    earlier = jnp.dot(lower, hits.astype(BF16), preferred_element_type=F32)
    meta = jnp.zeros((ROWS, META), F32)
    for k in range(topk):
        own = ids[:, k : k + 1]
        rank = jnp.sum(jnp.where(own == lane_f, earlier, 0.0), axis=1, keepdims=True)
        meta = jnp.where(lane == k, 2.0 * own + rank, meta)
        meta = jnp.where(lane == topk + k, gw[:, k : k + 1], meta)
    meta = meta.astype(BF16)

    for t in parts:
        mine = aligned(me[ORDERS[t][0]] * ROWS, ROWS)
        xs[t][mine, : widths[t]] = normed[:, offs[t] : offs[t] + widths[t]]
        xs[t][mine, widths[t] :] = meta

    pl.semaphore_wait(barrier, len(steps))

    sends = []

    def send(src, dst, sem, other):
        copy = pltpu.make_async_remote_copy(
            src, dst, send_sem, sem, device_id=device(other), device_id_type=MESH
        )
        copy.start()
        sends.append(copy)

    def arrive(ref, sem):
        pltpu.make_async_copy(ref, ref, sem).wait()

    def place(t, coords):
        _, b, c = ORDERS[t]
        return coords[b] * 4 + coords[c]

    def over_plane(half, t, src, dst, sem):
        _, b, c = ORDERS[t]
        here = place(t, me)
        for s0, s1 in PEERS:
            if (s0, s1, half) != (0, 0, 0):
                other = moved({b: s0, c: s1, "core": half})
                send(src.at[place(t, other)], dst.at[here], sem, other)
        if half == 0:
            dst[here] = src[here]

    def arrive_plane(half, ref, sem):
        arrive(ref.at[pl.ds(0, PLANE - 1 + half)], sem)

    for t in parts:
        a = ORDERS[t][0]
        mine = xs[t].at[aligned(me[a] * ROWS, ROWS)]
        for step in (1, 3, 2):
            send(mine, mine, p1_sem.at[t], moved({a: step}))

    for t in (1, 2):
        i, j = iota((HALF, HALF), 0), iota((HALF, HALF), 1)
        perm[t - 1] = jnp.where(arrival_index(t, i) == j, 1.0, 0.0).astype(BF16)
        perm_t[t - 1] = jnp.where(arrival_index(t, j) == i, 1.0, 0.0).astype(BF16)

    def slot_code(half, t, slot):
        _, b, c = ORDERS[t]
        base = dict(me)
        base[b], base[c] = 0, 0
        first = base["y"] * 32 + base["z"] * 8 + base["x"] * 2 + (base["core"] + half) % 2
        expert = first + slot // 32 * STRIDE[b] + slot // 8 % 4 * STRIDE[c]
        return (expert * 2 + slot % 2).astype(F32)

    def slots(half, t):
        rows = xs[t]
        info = rows[:, widths[t] :].astype(F32).T
        slot, row = iota((HALF, 64), 0), iota((HALF, 64), 1)
        code = slot_code(half, t, slot)
        hit = jnp.zeros((HALF, 64), F32)
        for k in range(topk):
            hit = jnp.where(info[k : k + 1, :] == code, 1.0, hit)
        hit = jnp.where(row // ROWS == slot % 8 // 2, hit, 0.0).astype(BF16)
        picked = jnp.dot(hit, rows[:, : widths[t]], preferred_element_type=F32).astype(BF16)
        n = half * 3 + t
        sb[n][...] = picked.reshape(PLANE, SLOTS, widths[t])
        over_plane(half, t, sb[n], ar[n], p2_sem.at[n])

    def weights_back(half, t):
        info = xs[t][:, widths[t] :].astype(F32)
        row, slot = iota((64, HALF), 0), iota((64, HALF), 1)
        code = slot_code(half, t, slot)
        weight = jnp.zeros((64, HALF), F32)
        for k in range(topk):
            weight = jnp.where(info[:, k : k + 1] == code, info[:, topk + k : topk + k + 1], weight)
        gates[half * 3 + t] = jnp.where(row // ROWS == slot % 8 // 2, weight, 0.0).astype(BF16)

    for t in parts:
        arrive(xs[t].at[pl.ds(0, 3 * ROWS)], p1_sem.at[t])
    for half in (0, 1):
        for t in parts:
            slots(half, t)
    for half in (0, 1):
        for t in parts:
            weights_back(half, t)

    units = gate_acc.shape[1]
    for half in (0, 1):
        if half == 0:
            loads[0].wait()
            loads[1].wait()
        for t in parts:
            n = half * 3 + t
            arrive_plane(half, ar[n], p2_sem.at[n])
            rows = ar[n][...].reshape(HALF, widths[t])
            if t > 0:
                rows = jnp.dot(perm[t - 1], rows, preferred_element_type=F32).astype(BF16)
            depth = pl.ds(offs[t], widths[t])
            for first in range(0, units, 512):
                cols = pl.ds(first, 512)
                for weights, total in ((wg, gate_acc), (wu, up_acc)):
                    part = jnp.dot(rows, weights[depth, cols], preferred_element_type=F32)
                    total[:, cols] = part if t == 0 else total[:, cols] + part

        gate = gate_acc[...]
        act[0] = (gate / (1.0 + jnp.exp(-gate)) * up_acc[...]).astype(BF16)

        if half == 0:
            loads[2].wait()
        for t in parts:
            n = half * 3 + t
            if t > 0:
                act[t] = jnp.dot(perm_t[t - 1], act[0], preferred_element_type=F32).astype(BF16)
            for first in range(0, widths[t], 256):
                wide = min(256, widths[t] - first)
                cols = pl.ds(offs[t] + first, wide)
                made = jnp.dot(act[t], wd[:, cols], preferred_element_type=F32).astype(BF16)
                ob[n][:, :, first : first + wide] = made.reshape(PLANE, SLOTS, wide)
            over_plane(half, t, ob[n], bk[n], r2_sem.at[n])

    for half in (0, 1):
        for t in parts:
            a = ORDERS[t][0]
            n = half * 3 + t
            arrive_plane(half, bk[n], r2_sem.at[n])
            back = bk[n][...].reshape(HALF, widths[t])
            summed = jnp.dot(gates[n], back, preferred_element_type=F32)
            if half == 0:
                pf[t][...] = summed
            else:
                summed = pf[t][...] + summed
                pf[t][...] = summed
                pb[t][...] = summed.astype(BF16)
                for step in (2, 1, 3):
                    other = moved({a: step})
                    send(pb[t].at[aligned(other[a] * ROWS, ROWS)], r1[t].at[step - 1], r1_sem.at[t], other)

    stores = []
    for t in parts:
        a = ORDERS[t][0]
        arrive(r1[t], r1_sem.at[t])
        total = pf[t][aligned(me[a] * ROWS, ROWS)]
        for k in range(3):
            total = total + r1[t][k].astype(F32)
        cols = pl.ds(offs[t], widths[t])
        out_ref[:, :, cols] = total.reshape(ROWS // 2, 2, widths[t]).astype(BF16)
        stores.append(pltpu.make_async_copy(out_ref.at[:, :, cols], out_hbm.at[:, :, cols], io_sem.at[t]))
        stores[-1].start()

    for store in stores:
        store.wait()
    for copy in sends:
        copy.wait_send()


def body(hidden, norm_gain, route_ids, gate_weights, w_gate, w_up, w_down):
    rows, steps, dmodel = hidden.shape
    topk = route_ids.shape[2]
    units = w_gate.shape[2]
    widths = part_widths(dmodel)
    count = rows * steps

    def each(rows_of, extra=0, kind=BF16, halves=2):
        return [pltpu.VMEM((*rows_of, w + extra), kind) for w in widths * halves]

    hbm = pl.BlockSpec(memory_space=pl.ANY)
    sem = pltpu.SemaphoreType.DMA
    result = pl.pallas_call(
        functools.partial(kernel, widths),
        out_shape=jax.ShapeDtypeStruct(hidden.shape, BF16),
        in_specs=[hbm] * 7,
        out_specs=hbm,
        scratch_shapes=[
            pltpu.VMEM(hidden.shape, BF16),
            pltpu.VMEM(norm_gain.shape, F32),
            pltpu.VMEM(route_ids.shape, jnp.int32),
            pltpu.VMEM(gate_weights.shape, F32),
            pltpu.VMEM(hidden.shape, BF16),
            pltpu.VMEM((dmodel, units), BF16),
            pltpu.VMEM((dmodel, units), BF16),
            pltpu.VMEM((units, dmodel), BF16),
            each((64,), META, halves=1),
            each((PLANE, SLOTS)),
            each((PLANE, SLOTS)),
            pltpu.VMEM((2, HALF, HALF), BF16),
            pltpu.VMEM((2, HALF, HALF), BF16),
            pltpu.VMEM((6, 64, HALF), BF16),
            pltpu.VMEM((HALF, units), F32),
            pltpu.VMEM((HALF, units), F32),
            pltpu.VMEM((3, HALF, units), BF16),
            each((PLANE, SLOTS)),
            each((PLANE, SLOTS)),
            each((64,), kind=F32, halves=1),
            each((64,), halves=1),
            each((3, ROWS), halves=1),
            sem((4,)),
            sem((3,)),
            sem,
            sem((3,)),
            sem((6,)),
            sem((6,)),
            sem((3,)),
        ],
        compiler_params=pltpu.CompilerParams(
            collective_id=0, has_side_effects=True, vmem_limit_bytes=56 * 2**20
        ),
        cost_estimate=pl.CostEstimate(
            flops=6 * 256 * dmodel * units, bytes_accessed=6 * dmodel * units, transcendentals=256 * units
        ),
    )(
        hidden,
        norm_gain,
        route_ids,
        gate_weights,
        w_gate,
        w_up,
        w_down,
    )
    return result


def solution(mesh):
    split = P(("grp", "ep"), None, None)
    return jax.shard_map(
        body,
        mesh=mesh,
        in_specs=(split, P(), split, split, split, split, split),
        out_specs=split,
        check_vma=False,
    )
```

time: 56.3 us -> 49.4 us (0.88)
  Pallas kernels: 54.5 us -> 47.7 us
    pallas_call x1, Pallas kernels: 54.5 us -> 47.7 us  [body(): pl.pallas_call(functools.partial(kernel, widths), out_shape=jax.ShapeDtyp...]
where the time goes in v3:
time: 49.4 us; the launch traced here: 49.3 us
  Pallas kernels  47.7 us (97%)
  local copies, waits for them, and re-layouts  1.62 us (3%)
    pallas_call x1, Pallas kernels, body(): pl.pallas_call(functools.partial(kernel, widths), out_shape=jax.ShapeDtyp...  47.7 us
    unnamed x1, local copies, waits for them, and re-layouts  1.62 us

profile of v3, /device:TPU:1, one launch (start us, length us, event | category | flops | bytes accessed | tf_op | source)
XLA Modules:
  0.0 49.3 jit_solution(17415060508570620658)
XLA Ops:
  0.0 47.7 %shard_map.73 = bf16[8,2,3584]{2,1,0:T(2,128)(2,1)} custom-call(bf16[8,2,3584]{2,1,0:T(2,128)(2,1)} %hid_hbm.1, f32[3584]{0:T(1024)} %gain_hbm.1, s32[8,2,8]{2,1,0:T(2,128)} %ids_hbm.1, f32[8,2,8]{2,1,0:T(2,128)} %gw_hbm.1, bf16[1,3584,1024]{2,1,0:T(8,128)(2,1)} %wg_hbm.1, bf16[1,3584,1024]{2,1,0:T(8,128)(2,1)} %wu_hbm.1, bf16[1,1024,3584]{2,1,0:T(8,128)(2,1)} %wd_hbm.1), custom_call_target="tpu_custom_call" | custom-call | flops 5637144576 | bytes 22020096 | tf_op jit(solution)/shard_map/pallas_call | solution.py:320
  47.7 1.6 %copy.9 = bf16[8,2,3584]{2,1,0:T(2,128)(2,1)} copy(bf16[8,2,3584]{2,1,0:T(2,128)(2,1)} %shard_map.73) | data formatting | bytes 229376

commit v4 on v3

--- a/solution.py
+++ b/solution.py
@@ -18,6 +18,7 @@
 PLANE = 16
 SLOTS = 8
 HALF = PLANE * SLOTS
+SPLIT = ((1, 2),)
 PEERS = [(i, j) for i in (2, 1, 3, 0) for j in (2, 1, 3, 0)]
 
 
@@ -86,10 +87,12 @@
     p2_sem,
     r2_sem,
     r1_sem,
+    out_sem,
 ):
     ep = lax.axis_index("ep")
     me = {"y": lax.axis_index("grp"), "z": ep // 8, "x": ep // 2 % 4, "core": ep % 2}
     parts = range(3)
+    sign = 1 + 2 * me["core"]
     offs = [sum(widths[:t]) for t in parts]
 
     def moved(steps):
@@ -172,12 +175,18 @@
         _, b, c = ORDERS[t]
         return coords[b] * 4 + coords[c]
 
+    def pieces(half, t):
+        if (half, t) in SPLIT:
+            first = (widths[t] // 2 + 64) // 128 * 128
+            return [(0, first), (first, widths[t] - first)]
+        return [(0, widths[t])]
+
     def over_plane(half, t, src, dst, sem):
         _, b, c = ORDERS[t]
         here = place(t, me)
         for s0, s1 in PEERS:
             if (s0, s1, half) != (0, 0, 0):
-                other = moved({b: s0, c: s1, "core": half})
+                other = moved({b: s0 * sign, c: s1 * sign, "core": half})
                 send(src.at[place(t, other)], dst.at[here], sem, other)
         if half == 0:
             dst[here] = src[here]
@@ -263,41 +272,50 @@
             n = half * 3 + t
             if t > 0:
                 act[t] = jnp.dot(perm_t[t - 1], act[0], preferred_element_type=F32).astype(BF16)
-            for first in range(0, widths[t], 256):
-                wide = min(256, widths[t] - first)
-                cols = pl.ds(offs[t] + first, wide)
-                made = jnp.dot(act[t], wd[:, cols], preferred_element_type=F32).astype(BF16)
-                ob[n][:, :, first : first + wide] = made.reshape(PLANE, SLOTS, wide)
-            over_plane(half, t, ob[n], bk[n], r2_sem.at[n])
+            for q, (left, size) in enumerate(pieces(half, t)):
+                for first in range(left, left + size, 256):
+                    wide = min(256, left + size - first)
+                    cols = pl.ds(offs[t] + first, wide)
+                    made = jnp.dot(act[t], wd[:, cols], preferred_element_type=F32).astype(BF16)
+                    ob[n][:, :, first : first + wide] = made.reshape(PLANE, SLOTS, wide)
+                cols = pl.ds(left, size)
+                over_plane(half, t, ob[n].at[:, :, cols], bk[n].at[:, :, cols], r2_sem.at[n, q])
 
     for half in (0, 1):
         for t in parts:
             a = ORDERS[t][0]
             n = half * 3 + t
-            arrive_plane(half, bk[n], r2_sem.at[n])
-            back = bk[n][...].reshape(HALF, widths[t])
-            summed = jnp.dot(gates[n], back, preferred_element_type=F32)
-            if half == 0:
-                pf[t][...] = summed
-            else:
-                summed = pf[t][...] + summed
-                pf[t][...] = summed
-                pb[t][...] = summed.astype(BF16)
-                for step in (2, 1, 3):
-                    other = moved({a: step})
-                    send(pb[t].at[aligned(other[a] * ROWS, ROWS)], r1[t].at[step - 1], r1_sem.at[t], other)
+            for q, (left, size) in enumerate(pieces(half, t)):
+                cols = pl.ds(left, size)
+                arrive_plane(half, bk[n].at[:, :, cols], r2_sem.at[n, q])
+                back = bk[n][:, :, cols].reshape(HALF, size)
+                summed = jnp.dot(gates[n], back, preferred_element_type=F32)
+                if half == 0:
+                    pf[t][:, cols] = summed
+                else:
+                    summed = pf[t][:, cols] + summed
+                    pf[t][:, cols] = summed
+                    pb[t][:, cols] = summed.astype(BF16)
+                    for step in (2, 1, 3):
+                        other = moved({a: step})
+                        src = pb[t].at[aligned(other[a] * ROWS, ROWS), cols]
+                        send(src, r1[t].at[step - 1, :, cols], r1_sem.at[t, q], other)
 
     stores = []
     for t in parts:
         a = ORDERS[t][0]
-        arrive(r1[t], r1_sem.at[t])
-        total = pf[t][aligned(me[a] * ROWS, ROWS)]
-        for k in range(3):
-            total = total + r1[t][k].astype(F32)
-        cols = pl.ds(offs[t], widths[t])
-        out_ref[:, :, cols] = total.reshape(ROWS // 2, 2, widths[t]).astype(BF16)
-        stores.append(pltpu.make_async_copy(out_ref.at[:, :, cols], out_hbm.at[:, :, cols], io_sem.at[t]))
-        stores[-1].start()
+        for q, (left, size) in enumerate(pieces(1, t)):
+            cols = pl.ds(left, size)
+            arrive(r1[t].at[:, :, cols], r1_sem.at[t, q])
+            total = pf[t][aligned(me[a] * ROWS, ROWS), cols]
+            for k in range(3):
+                total = total + r1[t][k, :, cols].astype(F32)
+            there = pl.ds(offs[t] + left, size)
+            out_ref[:, :, there] = total.reshape(ROWS // 2, 2, size).astype(BF16)
+            stores.append(
+                pltpu.make_async_copy(out_ref.at[:, :, there], out_hbm.at[:, :, there], out_sem.at[t, q])
+            )
+            stores[-1].start()
 
     for store in stores:
         store.wait()
@@ -350,8 +368,9 @@
             sem,
             sem((3,)),
             sem((6,)),
-            sem((6,)),
-            sem((3,)),
+            sem((6, 2)),
+            sem((3, 2)),
+            sem((3, 2)),
         ],
         compiler_params=pltpu.CompilerParams(
             collective_id=0, has_side_effects=True, vmem_limit_bytes=56 * 2**20

time: 49.4 us -> 48.9 us (0.990)
  Pallas kernels: 47.7 us -> 47.1 us
    pallas_call x1, Pallas kernels: 47.7 us -> 47.1 us  [body(): pl.pallas_call(functools.partial(kernel, widths), out_shape=jax.ShapeDtyp...]
where the time goes in v4:
time: 48.9 us; the launch traced here: 48.8 us
  Pallas kernels  47.1 us (96%)
  local copies, waits for them, and re-layouts  1.62 us (3%)
    pallas_call x1, Pallas kernels, body(): pl.pallas_call(functools.partial(kernel, widths), out_shape=jax.ShapeDtyp...  47.1 us
    unnamed x1, local copies, waits for them, and re-layouts  1.62 us

profile of v4, /device:TPU:1, one launch (start us, length us, event | category | flops | bytes accessed | tf_op | source)
XLA Modules:
  0.0 48.8 jit_solution(10134787466139481690)
XLA Ops:
  0.0 47.1 %shard_map.73 = bf16[8,2,3584]{2,1,0:T(2,128)(2,1)} custom-call(bf16[8,2,3584]{2,1,0:T(2,128)(2,1)} %hid_hbm.1, f32[3584]{0:T(1024)} %gain_hbm.1, s32[8,2,8]{2,1,0:T(2,128)} %ids_hbm.1, f32[8,2,8]{2,1,0:T(2,128)} %gw_hbm.1, bf16[1,3584,1024]{2,1,0:T(8,128)(2,1)} %wg_hbm.1, bf16[1,3584,1024]{2,1,0:T(8,128)(2,1)} %wu_hbm.1, bf16[1,1024,3584]{2,1,0:T(8,128)(2,1)} %wd_hbm.1), custom_call_target="tpu_custom_call" | custom-call | flops 5637144576 | bytes 22020096 | tf_op jit(solution)/shard_map/pallas_call | solution.py:338
  47.1 1.6 %copy.9 = bf16[8,2,3584]{2,1,0:T(2,128)(2,1)} copy(bf16[8,2,3584]{2,1,0:T(2,128)(2,1)} %shard_map.73) | data formatting | bytes 229376
